TPU v7x, 128 devices: a whole 4x4x4 slice. The times are simulated.
128 devices in a mesh: feat: 8 (over z, core), bulk: 16 (over y, x).
Axes of the slice: x: 4, y: 4, z: 4, core: 2. Of those that a mesh axis runs over, the one named last changes fastest.
Arguments:
- features: bfloat16 [262144, 4096], P('bulk', 'feat'), may hold values from -6 to 6
- project: bfloat16 [4096, 256], P('feat'), may hold values from -0.09375 to 0.09375
- bias: float32 [256], replicated, may hold values from -3 to 3
- send_rows: int32 [128, 128, 64], P(('feat', 'bulk')), may hold values from 0 to 2047
- send_count: int32 [128, 128], P(('feat', 'bulk')), may hold values from 0 to 64, as said below
- block_ids: int32 [128, 16, 12], P(('feat', 'bulk')), may hold values from 0 to 79, as said below
- block_weights: bfloat16 [128, 16, 12, 128, 128], P(('feat', 'bulk')), may hold values from 0 to 0.039794922
Outputs:
- node_states: bfloat16 [262144, 256], P(('bulk', 'feat'))
Inputs may be any that keep to these rules, and one draw needn't show every extreme that they name: `send_rows`: entries at or past a pair's count are valid row numbers that are not sent. `send_count`: some pair of devices has exactly 64 live rows. `block_ids`: the 12 blocks of one tile differ, and the tiles of one device together name every block of its buffer.
All inputs are finite; a program needn't handle non-finite values.
Results may differ from a plain program's by a relative error of at most 0.017.
Values may be sent and summed in bfloat16 or wider, within the bound.
A program may use at most 128 MiB of HBM per device.

v0:
```python
import jax
import jax.numpy as jnp
from jax import lax
from jax.sharding import PartitionSpec as P


def keep_live(values, counts):
    slots = jnp.arange(values.shape[-2], dtype=jnp.int32)
    live = slots < counts[..., None]
    return jnp.where(live[..., None], values, jnp.zeros_like(values))


def per_device(features, project, bias, send_rows, send_count, block_ids, block_weights):
    feat_count = lax.axis_size("feat")
    row_lists = send_rows[0]
    row_counts = send_count[0]
    device_total = row_lists.shape[0]
    cap_slots = row_lists.shape[1]
    hidden_width = project.shape[1]
    dest_rows = features.shape[0] // feat_count
    owned = lax.psum_scatter(
        jnp.dot(features, project, preferred_element_type=jnp.float32).astype(jnp.bfloat16),
        "feat",
        scatter_dimension=0,
        tiled=True,
    )
    outgoing = keep_live(owned[row_lists], row_counts)
    received = lax.all_to_all(outgoing, ("feat", "bulk"), split_axis=0, concat_axis=0, tiled=True)
    block_size = block_weights.shape[-1]
    buffer = jnp.concatenate(
        [owned, received.reshape(device_total * cap_slots, hidden_width)], axis=0
    )
    buffer = buffer.reshape(-1, block_size, hidden_width)
    sources = buffer[block_ids[0]]
    summed = jnp.einsum(
        "tkij,tkjh->tih", block_weights[0], sources, preferred_element_type=jnp.float32
    )
    return jax.nn.relu(summed.reshape(dest_rows, hidden_width) + bias).astype(jnp.bfloat16)


def solution(mesh):
    placed = (
        P("bulk", "feat"),
        P("feat", None),
        P(),
        P(("feat", "bulk"), None, None),
        P(("feat", "bulk"), None),
        P(("feat", "bulk"), None, None),
        P(("feat", "bulk"), None, None, None, None),
    )
    return jax.shard_map(
        per_device, mesh=mesh, in_specs=placed, out_specs=P(("bulk", "feat"), None), check_vma=False
    )
```

profile of v0, /device:TPU:1, one launch (start us, length us, event | category | flops | bytes accessed | tf_op | source)
XLA Modules:
  0.0 210.1 jit_solution(11768345416027878693)
XLA Ops:
  6.5 0.0 copy-start
  6.5 0.0 reduce-scatter.2.cloned.1.call-start
  6.5 0.9 copy-done
  7.5 13.5 %convolution_convert_fusion = bf16[16384,256]{1,0:T(8,128)(2,1)} fusion(bf16[16384,512]{1,0:T(8,128)(2,1)} %param.7, bf16[512,256]{1,0:T(8,128)(2,1)S(1)} %copy-done), kind=kOutput, calls=%fused_computation.2 | convolution fusion | flops 4299161600 | bytes 25427968 | tf_op jit(solution)/shard_map/dot_general | solution.py:22
  21.0 0.0 copy-start.2
  21.0 0.0 copy-start.5
  21.0 0.0 reduce-scatter.2.cloned.1.call-update
  21.0 0.7 copy-done.2
  21.8 0.1 copy.8
  21.9 0.1 reshape.95
  22.0 0.0 copy-done.5
  22.0 0.1 iota_compare_fusion
  22.1 54.3 %reduce-scatter.2.cloned.1.call-done = bf16[2048,256]{1,0:T(8,128)(2,1)} async-done(((bf16[16384,256]{1,0:T(8,128)(2,1)}), bf16[2048,256]{1,0:T(8,128)(2,1)}) %reduce-scatter.2.cloned.1.call-update) | async-done | bytes 1048592 | tf_op jit(solution)/shard_map/reduce_scatter | solution.py:21
  76.4 32.5 %gather_fusion = bf16[8192,256]{1,0:T(8,128)(2,1)} fusion(bf16[2048,256]{1,0:T(8,128)(2,1)} %reduce-scatter.2.cloned.1.call-done, s32[8192]{0:T(1024)S(1)} %broadcast_clamp_fusion), kind=kCustom, calls=%fused_computation | custom fusion | bytes 8421376 | tf_op jit(solution)/shard_map/gather | solution.py:27
  108.9 5.3 %broadcast_select_fusion = bf16[128,64,256]{2,1,0:T(8,128)(2,1)} fusion(bf16[128,64,256]{2,1,0:T(8,128)(2,1)} %bitcast.32, pred[128,64]{1,0:T(8,128)(4,1)S(1)} %iota_compare_fusion), kind=kLoop, calls=%fused_computation.6 | loop fusion | flops 2097152 | bytes 8396800 | tf_op jit(solution)/shard_map/jit(_where)/select_n | solution.py:10
  114.1 0.0 copy-start.3
  114.1 0.0 copy-start.1
  114.1 8.9 %all-to-all-start = ((bf16[128,64,256]{2,1,0:T(8,128)(2,1)}), bf16[128,64,256]{2,1,0:T(8,128)(2,1)}, u32[]{:S(2)}, u32[]{:S(2)}) async-start(bf16[128,64,256]{2,1,0:T(8,128)(2,1)} %broadcast_select_fusion), calls=%async_computation.1 | async-start | bytes 8388608 | tf_op jit(solution)/shard_map/all_to_all | solution.py:28
  123.0 0.0 copy-done.3
  123.1 0.1 copy.9
  123.1 0.1 reshape.103
  123.2 51.3 %all-to-all-done = bf16[128,64,256]{2,1,0:T(8,128)(2,1)} async-done(((bf16[128,64,256]{2,1,0:T(8,128)(2,1)}), bf16[128,64,256]{2,1,0:T(8,128)(2,1)}, u32[]{:S(2)}, u32[]{:S(2)}) %all-to-all-start) | async-done | bytes 4194336 | tf_op jit(solution)/shard_map/all_to_all | solution.py:28
  174.5 0.0 copy-done.1
  174.5 8.6 %pad_maximum_fusion = bf16[10240,256]{1,0:T(8,128)(2,1)} fusion(bf16[8192,256]{1,0:T(8,128)(2,1)} %bitcast.3, bf16[2048,256]{1,0:T(8,128)(2,1)S(1)} %copy-done.1), kind=kLoop, calls=%fused_computation.5 | loop fusion | flops 10485760 | bytes 10485760 | tf_op jit(solution)/shard_map/concatenate | solution.py:30
  183.1 10.7 %gather_fusion.1 = bf16[192,128,256]{2,1,0:T(8,128)(2,1)} fusion(bf16[80,128,256]{2,1,0:T(8,128)(2,1)} %bitcast.30, s32[1024]{0:T(1024)S(1)} %pad_clamp_fusion), kind=kCustom, calls=%fused_computation.1 | custom fusion | bytes 25166592 | tf_op jit(solution)/shard_map/gather | solution.py:34
  193.8 0.0 copy-start.4
  193.8 8.2 %fusion = f32[16,256,128,1]{1,2,3,0:T(8,128)S(1)} fusion(bf16[16,12,128,256]{3,2,1,0:T(8,128)(2,1)} %bitcast.31, bf16[1,16,12,128,128]{4,3,2,1,0:T(8,128)(2,1)} %param.13), kind=kOutput, calls=%fused_computation.3 | convolution fusion | flops 1610612736 | bytes 20971520 | tf_op jit(solution)/shard_map/tkij,tkjh->tih/dot_general | solution.py:35
  202.1 0.0 copy-done.4
  202.1 1.2 fusion.3
  (4 shorter events, 0.0 us)
Async XLA Ops:
  6.5 1.0 copy-start
  6.5 69.9 %reduce-scatter.2.cloned.1.call-start = ((), (), s32[]{:S(2)}) async-start(), calls=%async_computation.2 | async-start | bytes 9437184 | tf_op jit(solution)/shard_map/reduce_scatter | solution.py:21
  21.0 0.8 copy-start.2
  21.0 0.9 copy-start.5
  114.1 8.9 %copy-start.3 = (s32[1,16,12]{1,0,2:T(1,128)S(1)}, s32[1,16,12]{1,0,2:T(1,128)}, u32[]{:S(2)}) copy-start(s32[1,16,12]{1,0,2:T(1,128)} %param.12) | copy-start | bytes 2308
  114.1 60.4 %copy-start.1 = (bf16[2048,256]{1,0:T(8,128)(2,1)S(1)}, bf16[2048,256]{1,0:T(8,128)(2,1)}, u32[]{:S(2)}) copy-start(bf16[2048,256]{1,0:T(8,128)(2,1)} %reduce-scatter.2.cloned.1.call-done) | copy-start | bytes 3145732
  114.1 60.4 %all-to-all-start = ((bf16[128,64,256]{2,1,0:T(8,128)(2,1)}), bf16[128,64,256]{2,1,0:T(8,128)(2,1)}, u32[]{:S(2)}, u32[]{:S(2)}) async-start(bf16[128,64,256]{2,1,0:T(8,128)(2,1)} %broadcast_select_fusion), calls=%async_computation.1 | async-start | bytes 8388608 | tf_op jit(solution)/shard_map/all_to_all | solution.py:28
  193.8 8.2 %copy-start.4 = (f32[256]{0:T(256)S(1)}, f32[256]{0:T(256)}, u32[]{:S(2)}) copy-start(f32[256]{0:T(256)} %param.9) | copy-start | bytes 3076
Sparse Core Ops, SparseCore 0:
  21.2 55.1 reduce-scatter.1
where the time goes:
time: 211 us; the launch traced here: 210 us
  waiting for transfers between devices  106 us (50%)
  local copies, waits for them, and re-layouts  45.2 us (21%)
  matrix products  21.8 us (10%)
  other arithmetic  15.2 us (7%)
  between operations  13.5 us (6%)
  starting transfers between devices  8.89 us (4%)
    reduce_scatter x1, waiting for transfers between devices, per_device(): lax.psum_scatter(jnp.dot(features, project, preferred_element_type=jnp.fl...  54.3 us
    all_to_all x1, waiting for transfers between devices, per_device(): lax.all_to_all(outgoing, ('feat', 'bulk'), split_axis=0, concat_axis=0, t...  51.3 us
    gather x1, local copies, waits for them, and re-layouts, per_device(): outgoing = keep_live(owned[row_lists], row_counts)  32.5 us
    dot_general x1, matrix products, per_device(): jnp.dot(features, project, preferred_element_type=jnp.float32)  13.5 us
    gather x1, local copies, waits for them, and re-layouts, per_device(): sources = buffer[block_ids[0]]  10.7 us
    all_to_all x1, starting transfers between devices, per_device(): lax.all_to_all(outgoing, ('feat', 'bulk'), split_axis=0, concat_axis=0, t...  8.89 us
    concatenate x1, other arithmetic, per_device(): jnp.concatenate([owned, received.reshape(device_total * cap_slots, hidden...  8.59 us
    dot_general x1, matrix products, per_device(): jnp.einsum('tkij,tkjh->tih', block_weights[0], sources, preferred_element...  8.23 us
  transfers between devices with their start and end apart: 2, of which 2 were waited for; matrix products, arithmetic and copies ran while one was open for 0% of the time, Pallas kernels for 0%

commit v1 on v0

v1 whole, which is shorter than its diff:
```python
import jax
import jax.numpy as jnp
from jax import lax
from jax.experimental import pallas as pl
from jax.experimental.pallas import tpu as pltpu
from jax.sharding import PartitionSpec as P

MESH = pl.DeviceIdType.MESH

SIDE = 4
OWN = 2048
HALF = OWN // 2
PIECE = 256
PER_HALF = HALF // PIECE
UNITS = 2 * SIDE * PER_HALF
STAGE = 2 * PER_HALF
LAG = 4
SLOTS = 4
CAP = 64
HID = 256
DEV = 128
GROUP = 4
BLK = 128
STEP = 23


def rem(a, n):
    return lax.rem(a, jnp.int32(n))


def div(a, n):
    return lax.div(a, jnp.int32(n))


def kernel(
    x_hbm, w_ref, bias_ref, rows_ref, count_ref, ids_ref, bw_hbm, out_ref,
    xbuf, own, sib_out, sib_in, ring_in, buf, outgoing, weights, picks,
    x_sem, sib_send, sib_recv, ring_send, ring_recv, out_send, out_recv, self_sem, w_sem, meet,
):
    feat = lax.axis_index("feat")
    bulk = lax.axis_index("bulk")
    z, c = div(feat, 2), rem(feat, 2)
    y, x = div(bulk, SIDE), rem(bulk, SIDE)
    me = feat * 16 + bulk

    def at(dx, dy, dz, dc):
        return (
            rem(z + dz, SIDE) * 2 + rem(c + dc, 2),
            rem(y + dy, SIDE) * SIDE + rem(x + dx, SIDE),
        )

    sibling = at(0, 0, 0, 1)
    axis_pairs = (
        (at(1, 0, 0, 0), at(3, 0, 0, 0)),
        (at(0, 1, 0, 0), at(0, 3, 0, 0)),
        (at(0, 0, 1, 0), at(0, 0, 3, 0)),
    )
    rounds = (axis_pairs[0], axis_pairs[1], axis_pairs[1], axis_pairs[2], axis_pairs[2], (sibling,))

    def unit_place(u):
        stage, j, side = div(u, STAGE), rem(div(u, 2), PER_HALF), rem(u, 2)
        dz = jnp.where(stage == 0, 2, jnp.where(stage == 3, 0, 1 + 2 * side))
        half = jnp.where(stage == 1, 1 - side, side)
        return rem(z + dz, SIDE), half * HALF + j * PIECE

    def fetch(u):
        block, row = unit_place(u)
        slot = rem(u, SLOTS)
        return pltpu.make_async_copy(
            x_hbm.at[pl.ds(block * 2, 2), pl.ds(row, PIECE), :], xbuf.at[slot], x_sem.at[slot]
        )

    for u in range(SLOTS - 1):
        fetch(jnp.int32(u)).start()
    load_weights = pltpu.make_async_copy(bw_hbm, weights, w_sem)
    load_weights.start()

    barrier = pltpu.get_barrier_semaphore()
    neighbours = [sibling] + [d for pair in axis_pairs for d in pair]
    for d in neighbours:
        pl.semaphore_signal(barrier, inc=1, device_id=d, device_id_type=MESH)
    picked = rows_ref[...].astype(jnp.float32)
    slot_of = lax.broadcasted_iota(jnp.int32, (CAP, DEV), 0)
    picks[...] = jnp.where(slot_of < count_ref[...], picked, -1.0)
    pl.semaphore_wait(barrier, len(neighbours))

    def greet(r):
        for d in rounds[r]:
            pl.semaphore_signal(meet.at[r], inc=1, device_id=d, device_id_type=MESH)

    def greeted(r):
        pl.semaphore_wait(meet.at[r], len(rounds[r]))

    greet(0)

    def piece(u):
        return pl.ds(pl.multiple_of(u * PIECE, PIECE), PIECE)

    def to_sibling(u):
        return pltpu.make_async_remote_copy(
            src_ref=sib_out.at[piece(u)], dst_ref=sib_in.at[piece(u)],
            send_sem=sib_send, recv_sem=sib_recv.at[u], device_id=sibling, device_id_type=MESH,
        )

    def along(u):
        target = at(0, 0, 1 + 2 * rem(u, 2), 0)
        return pltpu.make_async_remote_copy(
            src_ref=own.at[piece(u)], dst_ref=ring_in.at[piece(u)],
            send_sem=ring_send, recv_sem=ring_recv.at[u], device_id=target, device_id_type=MESH,
        )

    def reduce_step(u, _):
        @pl.when(u < UNITS)
        def _():
            @pl.when(u + (SLOTS - 1) < UNITS)
            def _():
                fetch(u + (SLOTS - 1)).start()

            slot = rem(u, SLOTS)
            fetch(u).wait()
            sib_out[piece(u), :] = jnp.dot(
                xbuf[slot, 1 - c], w_ref[...], preferred_element_type=jnp.float32
            ).astype(jnp.bfloat16)
            to_sibling(u).start()
            own[piece(u), :] = jnp.dot(
                xbuf[slot, c], w_ref[...], preferred_element_type=jnp.float32
            ).astype(jnp.bfloat16)

        for r in range(len(rounds) - 1):
            @pl.when(u == 6 + 5 * r)
            def _():
                greeted(r)
                greet(r + 1)

        v = u - LAG

        @pl.when(v >= 0)
        def _():
            to_sibling(v).wait_recv()
            own[piece(v), :] = (
                own[piece(v), :].astype(jnp.float32) + sib_in[piece(v), :].astype(jnp.float32)
            ).astype(jnp.bfloat16)

            @pl.when(v < 2 * STAGE)
            def _():
                along(v).start()

        return 0

    lax.fori_loop(0, UNITS + LAG, reduce_step, 0)

    def relay_step(i, _):
        along(i).wait_recv()
        v = 2 * STAGE + i
        own[piece(v), :] = (
            own[piece(v), :].astype(jnp.float32) + ring_in[piece(i), :].astype(jnp.float32)
        ).astype(jnp.bfloat16)
        along(v).start()
        return 0

    lax.fori_loop(0, STAGE, relay_step, 0)
    greeted(len(rounds) - 1)

    def finish_step(i, _):
        side = rem(i, 2)
        direct, relayed, mine = STAGE + i + 1 - 2 * side, 2 * STAGE + i, 3 * STAGE + i
        along(direct).wait_recv()
        along(relayed).wait_recv()
        total = (
            own[piece(mine), :].astype(jnp.float32)
            + ring_in[piece(direct), :].astype(jnp.float32)
            + ring_in[piece(relayed), :].astype(jnp.float32)
        )
        block = (side * HALF + div(i, 2) * PIECE) // BLK
        buf[pl.ds(block, PIECE // BLK)] = total.astype(jnp.bfloat16).reshape(PIECE // BLK, BLK, HID)
        return 0

    lax.fori_loop(0, STAGE, finish_step, 0)

    lane = lax.broadcasted_iota(jnp.int32, (CAP, DEV), 1)
    node = lax.broadcasted_iota(jnp.int32, (GROUP * CAP, PIECE), 1).astype(jnp.float32)
    landing = buf.at[OWN // BLK + div(me, 2), pl.ds(pl.multiple_of(rem(me, 2) * CAP, CAP), CAP)]

    def receiver(k):
        v = jnp.where(k < DEV - 1, 1 + rem(STEP * k, DEV - 1), 0)
        return at(rem(v, 4), rem(div(v, 4), 4), div(v, 32), rem(div(v, 16), 2))

    def send(k):
        return pltpu.make_async_remote_copy(
            src_ref=outgoing.at[pl.ds(pl.multiple_of(k * CAP, CAP), CAP)],
            dst_ref=landing,
            send_sem=out_send, recv_sem=out_recv, device_id=receiver(k), device_id_type=MESH,
        )

    def gather_step(g, _):
        columns = []
        for q in range(GROUP):
            to_feat, to_bulk = receiver(g * GROUP + q)
            chosen = lane == to_feat * 16 + to_bulk
            columns.append(jnp.sum(jnp.where(chosen, picks[...], 0.0), axis=1, keepdims=True))
        column = jnp.concatenate(columns, axis=0)
        rows = jnp.zeros((GROUP * CAP, HID), jnp.float32)
        for t in range(OWN // PIECE):
            hot = jnp.where(column - float(t * PIECE) == node, 1.0, 0.0).astype(jnp.bfloat16)
            rows += jnp.dot(
                hot, buf[2 * t:2 * t + 2].reshape(PIECE, HID), preferred_element_type=jnp.float32
            )
        start = pl.multiple_of(g * (GROUP * CAP), GROUP * CAP)
        outgoing[pl.ds(start, GROUP * CAP), :] = rows.astype(jnp.bfloat16)
        for q in range(GROUP - 1):
            send(g * GROUP + q).start()

        @pl.when(g < DEV // GROUP - 1)
        def _():
            send(g * GROUP + GROUP - 1).start()

        return 0

    lax.fori_loop(0, DEV // GROUP, gather_step, 0)
    last = pltpu.make_async_copy(
        outgoing.at[pl.ds((DEV - 1) * CAP, CAP)], landing, self_sem
    )
    last.start()
    last.wait()
    sent = outgoing.at[pl.ds(0, (DEV - 1) * CAP)]
    pltpu.make_async_copy(sent, sent, out_recv).wait()
    load_weights.wait()

    def tile_step(t, _):
        total = jnp.zeros((BLK, HID), jnp.float32)
        for k in range(0, 12, 2):
            blocks = [buf[ids_ref[k, t]], buf[ids_ref[k + 1, t]]]
            total += jnp.dot(
                jnp.concatenate([weights[t, k], weights[t, k + 1]], axis=1),
                jnp.concatenate(blocks, axis=0),
                preferred_element_type=jnp.float32,
            )
        row = pl.multiple_of(t * BLK, BLK)
        out_ref[pl.ds(row, BLK), :] = jnp.maximum(total + bias_ref[...], 0.0).astype(jnp.bfloat16)
        return 0

    lax.fori_loop(0, 16, tile_step, 0)

    pltpu.make_async_copy(sent, sent, out_send).wait()
    pltpu.make_async_copy(sib_out, sib_out, sib_send).wait()
    ringed = own.at[pl.ds(0, 3 * STAGE * PIECE)]
    pltpu.make_async_copy(ringed, ringed, ring_send).wait()


def per_device(features, project, bias, send_rows, send_count, block_ids, block_weights):
    vmem = pl.BlockSpec(memory_space=pltpu.VMEM)
    anywhere = pl.BlockSpec(memory_space=pl.ANY)
    bf16 = jnp.bfloat16
    return pl.pallas_call(
        kernel,
        out_shape=jax.ShapeDtypeStruct((OWN, HID), bf16),
        in_specs=[
            anywhere, vmem, vmem, vmem, vmem, pl.BlockSpec(memory_space=pltpu.SMEM), anywhere,
        ],
        out_specs=vmem,
        scratch_shapes=[
            pltpu.VMEM((SLOTS, 2, PIECE, 512), bf16),
            pltpu.VMEM((UNITS * PIECE, HID), bf16),
            pltpu.VMEM((UNITS * PIECE, HID), bf16),
            pltpu.VMEM((UNITS * PIECE, HID), bf16),
            pltpu.VMEM((3 * STAGE * PIECE, HID), bf16),
            pltpu.VMEM(((OWN + DEV * CAP) // BLK, BLK, HID), bf16),
            pltpu.VMEM((DEV * CAP, HID), bf16),
            pltpu.VMEM((16, 12, BLK, BLK), bf16),
            pltpu.VMEM((CAP, DEV), jnp.float32),
            pltpu.SemaphoreType.DMA((SLOTS,)),
            pltpu.SemaphoreType.DMA,
            pltpu.SemaphoreType.DMA((UNITS,)),
            pltpu.SemaphoreType.DMA,
            pltpu.SemaphoreType.DMA((3 * STAGE,)),
            pltpu.SemaphoreType.DMA,
            pltpu.SemaphoreType.DMA,
            pltpu.SemaphoreType.DMA,
            pltpu.SemaphoreType.DMA,
            pltpu.SemaphoreType.REGULAR((6,)),
        ],
        compiler_params=pltpu.CompilerParams(
            collective_id=0, has_side_effects=True, vmem_limit_bytes=56 * 1024 * 1024
        ),
        cost_estimate=pl.CostEstimate(
            flops=15_000_000_000, bytes_accessed=24 * 1024 * 1024, transcendentals=0
        ),
    )(
        features.reshape(8, OWN, 512), project, bias.reshape(1, HID), send_rows[0].T, send_count,
        block_ids[0].T, block_weights[0],
    )


def solution(mesh):
    placed = (
        P("bulk", "feat"),
        P("feat", None),
        P(),
        P(("feat", "bulk"), None, None),
        P(("feat", "bulk"), None),
        P(("feat", "bulk"), None, None),
        P(("feat", "bulk"), None, None, None, None),
    )
    return jax.shard_map(
        per_device, mesh=mesh, in_specs=placed, out_specs=P(("bulk", "feat"), None), check_vma=False
    )
```

time: 211 us -> 106 us (0.50)
  waiting for transfers between devices: 106 us -> 0 us
  Pallas kernels: 0 us -> 103 us
  local copies, waits for them, and re-layouts: 45.2 us -> 3.55 us
  matrix products: 21.8 us -> 0 us
  other arithmetic: 15.2 us -> 0 us
  between operations: 13.5 us -> 0.01 us
  starting transfers between devices: 8.89 us -> 0 us
    pallas_call x0 -> x1, Pallas kernels: none -> 103 us  [per_device(): pl.pallas_call(kernel, out_shape=jax.ShapeDtypeStruct((OWN, HID), bf16),...]
    reduce_scatter x1 -> x0, waiting for transfers between devices: 54.3 us -> none  [per_device(): lax.psum_scatter(jnp.dot(features, project, preferred_element_type=jnp.fl...]
    all_to_all x1 -> x0, waiting for transfers between devices: 51.3 us -> none  [per_device(): lax.all_to_all(outgoing, ('feat', 'bulk'), split_axis=0, concat_axis=0, t...]
    gather x2 -> x0, local copies, waits for them, and re-layouts: 43.2 us -> none  [the longest x1 32.5 us: per_device(): outgoing = keep_live(owned[row_lists], row_counts)]
    dot_general x2 -> x0, matrix products: 21.8 us -> none  [the longest x1 13.5 us: per_device(): jnp.dot(features, project, preferred_element_type=jnp.float32)]
    all_to_all x1 -> x0, starting transfers between devices: 8.89 us -> none  [per_device(): lax.all_to_all(outgoing, ('feat', 'bulk'), split_axis=0, concat_axis=0, t...]
    concatenate x1 -> x0, other arithmetic: 8.59 us -> none  [per_device(): jnp.concatenate([owned, received.reshape(device_total * cap_slots, hidden...]
    select_n x3 -> x0, other arithmetic: 5.29 us -> none  [the longest x1 5.27 us: keep_live(): return jnp.where(live[..., None], values, jnp.zeros_like(values))]
  transfers between devices with their start and end apart: 2 -> 0, of which waited for: 2 -> 0; matrix products, arithmetic and copies ran while one was open for 0% -> 0% of each run, Pallas kernels for 0% -> 0%
where the time goes in v1:
time: 106 us
  Pallas kernels  103 us (97%)
  local copies, waits for them, and re-layouts  3.55 us (3%)
    pallas_call x1, Pallas kernels, per_device(): pl.pallas_call(kernel, out_shape=jax.ShapeDtypeStruct((OWN, HID), bf16),...  103 us
    unnamed x2, local copies, waits for them, and re-layouts  3.55 us

profile of v1, /device:TPU:1, one launch (start us, length us, event | category | flops | bytes accessed | tf_op | source)
XLA Modules:
  0.0 106.1 jit_solution(6832057611982432654)
XLA Ops:
  0.0 1.3 %copy.10 = s32[1,16,12]{1,2,0:T(8,128)} copy(s32[1,16,12]{1,0,2:T(1,128)} %param.12) | data formatting | bytes 1536
  1.3 102.5 %shard_map.73 = bf16[2048,256]{1,0:T(8,128)(2,1)} custom-call(bf16[8,2048,512]{2,1,0:T(8,128)(2,1)} %bitcast.12, bf16[512,256]{1,0:T(8,128)(2,1)} %w_ref.1, f32[1,256]{1,0:T(1,128)} %bitcast.15, s32[64,128]{1,0:T(8,128)} %bitcast.14, s32[1,128]{1,0:T(1,128)} %count_ref.1, s32[12,16]{1,0:T(8,128)} %bitcast.11, bf16[16,12,128,128]{3,2,1,0:T(8,128)(2,1)} %bitcast.13), custom_call_target="tpu_custom_call" | custom-call | flops 15000000512 | bytes 25165824 | tf_op jit(solution)/shard_map/pallas_call | solution.py:254
  103.8 2.3 %copy.12 = bf16[2048,256]{1,0:T(8,128)(2,1)} copy(bf16[2048,256]{1,0:T(8,128)(2,1)} %shard_map.73) | data formatting | bytes 2097152

commit v2 on v1

--- a/solution.py
+++ b/solution.py
@@ -14,13 +14,15 @@
 PER_HALF = HALF // PIECE
 UNITS = 2 * SIDE * PER_HALF
 STAGE = 2 * PER_HALF
-LAG = 4
+LAG = 3
+EARLY = 3
 SLOTS = 4
 CAP = 64
 HID = 256
 DEV = 128
 GROUP = 4
 BLK = 128
+TOGETHER = 4
 STEP = 23
 
 
@@ -50,12 +52,10 @@
         )
 
     sibling = at(0, 0, 0, 1)
-    axis_pairs = (
-        (at(1, 0, 0, 0), at(3, 0, 0, 0)),
-        (at(0, 1, 0, 0), at(0, 3, 0, 0)),
-        (at(0, 0, 1, 0), at(0, 0, 3, 0)),
-    )
-    rounds = (axis_pairs[0], axis_pairs[1], axis_pairs[1], axis_pairs[2], axis_pairs[2], (sibling,))
+    along_x = [at(d, 0, 0, 0) for d in range(1, SIDE)]
+    along_y = [at(0, d, 0, 0) for d in range(1, SIDE)]
+    along_z = [at(0, 0, d, 0) for d in range(1, SIDE)]
+    rounds = (along_x, along_z, [sibling])
 
     def unit_place(u):
         stage, j, side = div(u, STAGE), rem(div(u, 2), PER_HALF), rem(u, 2)
@@ -66,23 +66,25 @@
     def fetch(u):
         block, row = unit_place(u)
         slot = rem(u, SLOTS)
-        return pltpu.make_async_copy(
-            x_hbm.at[pl.ds(block * 2, 2), pl.ds(row, PIECE), :], xbuf.at[slot], x_sem.at[slot]
-        )
+        return [
+            pltpu.make_async_copy(
+                x_hbm.at[block * 2 + e, pl.ds(row, PIECE), :], xbuf.at[slot, i], x_sem.at[slot]
+            )
+            for i, e in enumerate((c, 1 - c))
+        ]
 
     for u in range(SLOTS - 1):
-        fetch(jnp.int32(u)).start()
+        for f in fetch(jnp.int32(u)):
+            f.start()
     load_weights = pltpu.make_async_copy(bw_hbm, weights, w_sem)
-    load_weights.start()
 
     barrier = pltpu.get_barrier_semaphore()
-    neighbours = [sibling] + [d for pair in axis_pairs for d in pair]
+    neighbours = [sibling] + along_x + along_y + along_z
     for d in neighbours:
         pl.semaphore_signal(barrier, inc=1, device_id=d, device_id_type=MESH)
     picked = rows_ref[...].astype(jnp.float32)
     slot_of = lax.broadcasted_iota(jnp.int32, (CAP, DEV), 0)
     picks[...] = jnp.where(slot_of < count_ref[...], picked, -1.0)
-    pl.semaphore_wait(barrier, len(neighbours))
 
     def greet(r):
         for d in rounds[r]:
@@ -90,8 +92,6 @@
 
     def greeted(r):
         pl.semaphore_wait(meet.at[r], len(rounds[r]))
-
-    greet(0)
 
     def piece(u):
         return pl.ds(pl.multiple_of(u * PIECE, PIECE), PIECE)
@@ -109,25 +109,39 @@
             send_sem=ring_send, recv_sem=ring_recv.at[u], device_id=target, device_id_type=MESH,
         )
 
+    def product(u):
+        @pl.when(u + (SLOTS - 1) < UNITS)
+        def _():
+            for f in fetch(u + (SLOTS - 1)):
+                f.start()
+
+        slot = rem(u, SLOTS)
+        pltpu.make_async_copy(xbuf.at[slot], xbuf.at[slot], x_sem.at[slot]).wait()
+        both = jnp.dot(
+            xbuf[slot].reshape(2 * PIECE, 512), w_ref[...], preferred_element_type=jnp.float32
+        ).astype(jnp.bfloat16)
+        sib_out[piece(u), :] = both[PIECE:]
+        own[piece(u), :] = both[:PIECE]
+
+    def early_step(u, _):
+        product(u)
+        return 0
+
+    lax.fori_loop(0, EARLY, early_step, 0)
+    pl.semaphore_wait(barrier, len(neighbours))
+    for u in range(EARLY):
+        to_sibling(jnp.int32(u)).start()
+    greet(0)
+    load_weights.start()
+
     def reduce_step(u, _):
         @pl.when(u < UNITS)
         def _():
-            @pl.when(u + (SLOTS - 1) < UNITS)
-            def _():
-                fetch(u + (SLOTS - 1)).start()
-
-            slot = rem(u, SLOTS)
-            fetch(u).wait()
-            sib_out[piece(u), :] = jnp.dot(
-                xbuf[slot, 1 - c], w_ref[...], preferred_element_type=jnp.float32
-            ).astype(jnp.bfloat16)
+            product(u)
             to_sibling(u).start()
-            own[piece(u), :] = jnp.dot(
-                xbuf[slot, c], w_ref[...], preferred_element_type=jnp.float32
-            ).astype(jnp.bfloat16)
 
         for r in range(len(rounds) - 1):
-            @pl.when(u == 6 + 5 * r)
+            @pl.when(u == 12 + 8 * r)
             def _():
                 greeted(r)
                 greet(r + 1)
@@ -147,7 +161,7 @@
 
         return 0
 
-    lax.fori_loop(0, UNITS + LAG, reduce_step, 0)
+    lax.fori_loop(EARLY, UNITS + LAG, reduce_step, 0)
 
     def relay_step(i, _):
         along(i).wait_recv()
@@ -178,7 +192,7 @@
     lax.fori_loop(0, STAGE, finish_step, 0)
 
     lane = lax.broadcasted_iota(jnp.int32, (CAP, DEV), 1)
-    node = lax.broadcasted_iota(jnp.int32, (GROUP * CAP, PIECE), 1).astype(jnp.float32)
+    node = lax.broadcasted_iota(jnp.int32, (GROUP * CAP, PIECE), 1).astype(jnp.bfloat16)
     landing = buf.at[OWN // BLK + div(me, 2), pl.ds(pl.multiple_of(rem(me, 2) * CAP, CAP), CAP)]
 
     def receiver(k):
@@ -201,7 +215,9 @@
         column = jnp.concatenate(columns, axis=0)
         rows = jnp.zeros((GROUP * CAP, HID), jnp.float32)
         for t in range(OWN // PIECE):
-            hot = jnp.where(column - float(t * PIECE) == node, 1.0, 0.0).astype(jnp.bfloat16)
+            near = column - float(t * PIECE)
+            near = jnp.where((near >= 0.0) & (near < float(PIECE)), near, -1.0).astype(jnp.bfloat16)
+            hot = jnp.where(near == node, jnp.bfloat16(1), jnp.bfloat16(0))
             rows += jnp.dot(
                 hot, buf[2 * t:2 * t + 2].reshape(PIECE, HID), preferred_element_type=jnp.float32
             )
@@ -226,20 +242,22 @@
     pltpu.make_async_copy(sent, sent, out_recv).wait()
     load_weights.wait()
 
-    def tile_step(t, _):
-        total = jnp.zeros((BLK, HID), jnp.float32)
-        for k in range(0, 12, 2):
-            blocks = [buf[ids_ref[k, t]], buf[ids_ref[k + 1, t]]]
-            total += jnp.dot(
-                jnp.concatenate([weights[t, k], weights[t, k + 1]], axis=1),
-                jnp.concatenate(blocks, axis=0),
-                preferred_element_type=jnp.float32,
-            )
-        row = pl.multiple_of(t * BLK, BLK)
-        out_ref[pl.ds(row, BLK), :] = jnp.maximum(total + bias_ref[...], 0.0).astype(jnp.bfloat16)
-        return 0
-
-    lax.fori_loop(0, 16, tile_step, 0)
+    def tile_step(i, _):
+        for e in range(TOGETHER):
+            t = i * TOGETHER + e
+            total = jnp.zeros((BLK, HID), jnp.float32)
+            for k in range(0, 12, 2):
+                blocks = [buf[ids_ref[k, 0, t]], buf[ids_ref[k + 1, 0, t]]]
+                total += jnp.dot(
+                    jnp.concatenate([weights[t, k], weights[t, k + 1]], axis=1),
+                    jnp.concatenate(blocks, axis=0),
+                    preferred_element_type=jnp.float32,
+                )
+            row = pl.multiple_of(t * BLK, BLK)
+            out_ref[pl.ds(row, BLK), :] = (total + bias_ref[...]).astype(jnp.bfloat16)
+        return 0
+
+    lax.fori_loop(0, 16 // TOGETHER, tile_step, 0)
 
     pltpu.make_async_copy(sent, sent, out_send).wait()
     pltpu.make_async_copy(sib_out, sib_out, sib_send).wait()
@@ -251,7 +269,7 @@
     vmem = pl.BlockSpec(memory_space=pltpu.VMEM)
     anywhere = pl.BlockSpec(memory_space=pl.ANY)
     bf16 = jnp.bfloat16
-    return pl.pallas_call(
+    summed = pl.pallas_call(
         kernel,
         out_shape=jax.ShapeDtypeStruct((OWN, HID), bf16),
         in_specs=[
@@ -277,7 +295,7 @@
             pltpu.SemaphoreType.DMA,
             pltpu.SemaphoreType.DMA,
             pltpu.SemaphoreType.DMA,
-            pltpu.SemaphoreType.REGULAR((6,)),
+            pltpu.SemaphoreType.REGULAR((3,)),
         ],
         compiler_params=pltpu.CompilerParams(
             collective_id=0, has_side_effects=True, vmem_limit_bytes=56 * 1024 * 1024
@@ -287,8 +305,9 @@
         ),
     )(
         features.reshape(8, OWN, 512), project, bias.reshape(1, HID), send_rows[0].T, send_count,
-        block_ids[0].T, block_weights[0],
+        block_ids.transpose(2, 0, 1), block_weights[0],
     )
+    return jnp.maximum(summed, 0)
 
 
 def solution(mesh):

time: 106 us -> 102 us (0.962)
  local copies, waits for them, and re-layouts: 3.55 us -> 0 us
  Pallas kernels: 103 us -> 99.7 us
  other arithmetic: 0 us -> 2.26 us
    unnamed x2 -> x0, local copies, waits for them, and re-layouts: 3.55 us -> none
    pallas_call x1, Pallas kernels: 103 us -> 99.7 us  [per_device(): pl.pallas_call(kernel, out_shape=jax.ShapeDtypeStruct((OWN, HID), bf16),...]
    max x0 -> x1, other arithmetic: none -> 2.26 us  [per_device(): return jnp.maximum(summed, 0)]
where the time goes in v2:
time: 102 us
  Pallas kernels  99.7 us (98%)
  other arithmetic  2.26 us (2%)
    pallas_call x1, Pallas kernels, per_device(): pl.pallas_call(kernel, out_shape=jax.ShapeDtypeStruct((OWN, HID), bf16),...  99.7 us
    max x1, other arithmetic, per_device(): return jnp.maximum(summed, 0)  2.26 us

profile of v2, /device:TPU:1, one launch (start us, length us, event | category | flops | bytes accessed | tf_op | source)
XLA Modules:
  0.0 102.0 jit_solution(7011150179973423803)
XLA Ops:
  0.0 99.7 %shard_map.73 = bf16[2048,256]{1,0:T(8,128)(2,1)} custom-call(bf16[8,2048,512]{2,1,0:T(8,128)(2,1)} %bitcast.7, bf16[512,256]{1,0:T(8,128)(2,1)} %w_ref.1, f32[1,256]{1,0:T(1,128)} %bitcast.11, s32[64,128]{1,0:T(8,128)} %bitcast.9, s32[1,128]{1,0:T(1,128)} %count_ref.1, s32[12,1,16]{2,1,0:T(1,128)} %bitcast.10, bf16[16,12,128,128]{3,2,1,0:T(8,128)(2,1)} %bitcast.8), custom_call_target="tpu_custom_call" | custom-call | flops 15000000512 | bytes 25165824 | tf_op jit(solution)/shard_map/pallas_call | solution.py:272
  99.7 2.3 %broadcast_maximum_fusion = bf16[2048,256]{1,0:T(8,128)(2,1)} fusion(bf16[2048,256]{1,0:T(8,128)(2,1)} %shard_map.73), kind=kLoop, calls=%fused_computation | loop fusion | flops 524288 | bytes 2097152 | tf_op jit(solution)/shard_map/max | solution.py:310

commit v3 on v2

--- a/solution.py
+++ b/solution.py
@@ -14,15 +14,15 @@
 PER_HALF = HALF // PIECE
 UNITS = 2 * SIDE * PER_HALF
 STAGE = 2 * PER_HALF
-LAG = 3
-EARLY = 3
+LAG = 2
+EARLY = 2
 SLOTS = 4
 CAP = 64
 HID = 256
 DEV = 128
 GROUP = 4
 BLK = 128
-TOGETHER = 4
+TOGETHER = 8
 STEP = 23
 
 
@@ -298,7 +298,7 @@
             pltpu.SemaphoreType.REGULAR((3,)),
         ],
         compiler_params=pltpu.CompilerParams(
-            collective_id=0, has_side_effects=True, vmem_limit_bytes=56 * 1024 * 1024
+            collective_id=0, has_side_effects=True, vmem_limit_bytes=50 * 1024 * 1024
         ),
         cost_estimate=pl.CostEstimate(
             flops=15_000_000_000, bytes_accessed=24 * 1024 * 1024, transcendentals=0

time: 102 us -> 103 us (level)
  local copies, waits for them, and re-layouts: 0 us -> 3.73 us
  Pallas kernels: 99.7 us -> 98.1 us
  other arithmetic: 2.26 us -> 1.04 us
    unnamed x0 -> x10, local copies, waits for them, and re-layouts: none -> 3.73 us
    pallas_call x1, Pallas kernels: 99.7 us -> 98.1 us  [per_device(): pl.pallas_call(kernel, out_shape=jax.ShapeDtypeStruct((OWN, HID), bf16),...]
    max x1, other arithmetic: 2.26 us -> 1.04 us  [per_device(): return jnp.maximum(summed, 0)]
where the time goes in v3:
time: 103 us
  Pallas kernels  98.1 us (95%)
  local copies, waits for them, and re-layouts  3.73 us (4%)
  other arithmetic  1.04 us (1%)
    pallas_call x1, Pallas kernels, per_device(): pl.pallas_call(kernel, out_shape=jax.ShapeDtypeStruct((OWN, HID), bf16),...  98.1 us
    unnamed x10, local copies, waits for them, and re-layouts  3.73 us

profile of v3, /device:TPU:1, one launch (start us, length us, event | category | flops | bytes accessed | tf_op | source)
XLA Modules:
  0.0 102.9 jit_solution(17379198307128260601)
XLA Ops:
  0.0 0.0 copy-start
  0.0 0.9 copy-done
  1.0 0.0 copy-start.1
  1.0 0.8 copy-done.1
  1.7 0.0 copy-start.2
  1.7 0.7 copy-done.2
  2.4 0.0 copy-start.3
  2.4 0.7 copy-done.3
  3.1 0.0 copy-start.4
  3.1 0.7 copy-done.4
  3.7 98.1 %shard_map.73 = bf16[2048,256]{1,0:T(8,128)(2,1)S(1)} custom-call(bf16[8,2048,512]{2,1,0:T(8,128)(2,1)} %bitcast.10, bf16[512,256]{1,0:T(8,128)(2,1)S(1)} %copy-done, f32[1,256]{1,0:T(1,128)S(1)} %bitcast.9, s32[64,128]{1,0:T(8,128)S(1)} %bitcast.7, s32[1,128]{1,0:T(1,128)S(1)} %copy-done.4, s32[12,1,16]{2,1,0:T(1,128)S(1)} %bitcast.8, ...), custom_call_target="tpu_custom_call" | custom-call | flops 15000000512 | bytes 25165824 | tf_op jit(solution)/shard_map/pallas_call | solution.py:272
  101.9 1.0 %broadcast_maximum_fusion = bf16[2048,256]{1,0:T(8,128)(2,1)} fusion(bf16[2048,256]{1,0:T(8,128)(2,1)S(1)} %shard_map.73), kind=kLoop, calls=%fused_computation | loop fusion | flops 524288 | bytes 2097152 | tf_op jit(solution)/shard_map/max | solution.py:310
Async XLA Ops:
  0.0 0.9 copy-start
  1.0 0.8 copy-start.1
  1.7 0.7 copy-start.2
  2.4 0.7 copy-start.3
  3.1 0.7 copy-start.4

commit v4 on v3

--- a/solution.py
+++ b/solution.py
@@ -298,7 +298,7 @@
             pltpu.SemaphoreType.REGULAR((3,)),
         ],
         compiler_params=pltpu.CompilerParams(
-            collective_id=0, has_side_effects=True, vmem_limit_bytes=50 * 1024 * 1024
+            collective_id=0, has_side_effects=True, vmem_limit_bytes=56 * 1024 * 1024
         ),
         cost_estimate=pl.CostEstimate(
             flops=15_000_000_000, bytes_accessed=24 * 1024 * 1024, transcendentals=0

time: 103 us -> 102 us (level)
  local copies, waits for them, and re-layouts: 3.73 us -> 0 us
  Pallas kernels: 98.1 us -> 99.5 us
  other arithmetic: 1.04 us -> 2.26 us
    unnamed x10 -> x0, local copies, waits for them, and re-layouts: 3.73 us -> none
    pallas_call x1, Pallas kernels: 98.1 us -> 99.5 us  [per_device(): pl.pallas_call(kernel, out_shape=jax.ShapeDtypeStruct((OWN, HID), bf16),...]
    max x1, other arithmetic: 1.04 us -> 2.26 us  [per_device(): return jnp.maximum(summed, 0)]
where the time goes in v4:
time: 102 us
  Pallas kernels  99.5 us (98%)
  other arithmetic  2.26 us (2%)
    pallas_call x1, Pallas kernels, per_device(): pl.pallas_call(kernel, out_shape=jax.ShapeDtypeStruct((OWN, HID), bf16),...  99.5 us
    max x1, other arithmetic, per_device(): return jnp.maximum(summed, 0)  2.26 us

profile of v4, /device:TPU:1, one launch (start us, length us, event | category | flops | bytes accessed | tf_op | source)
XLA Modules:
  0.0 101.7 jit_solution(2229974348715116075)
XLA Ops:
  0.0 99.5 %shard_map.73 = bf16[2048,256]{1,0:T(8,128)(2,1)} custom-call(bf16[8,2048,512]{2,1,0:T(8,128)(2,1)} %bitcast.7, bf16[512,256]{1,0:T(8,128)(2,1)} %w_ref.1, f32[1,256]{1,0:T(1,128)} %bitcast.11, s32[64,128]{1,0:T(8,128)} %bitcast.9, s32[1,128]{1,0:T(1,128)} %count_ref.1, s32[12,1,16]{2,1,0:T(1,128)} %bitcast.10, bf16[16,12,128,128]{3,2,1,0:T(8,128)(2,1)} %bitcast.8), custom_call_target="tpu_custom_call" | custom-call | flops 15000000512 | bytes 25165824 | tf_op jit(solution)/shard_map/pallas_call | solution.py:272
  99.5 2.3 %broadcast_maximum_fusion = bf16[2048,256]{1,0:T(8,128)(2,1)} fusion(bf16[2048,256]{1,0:T(8,128)(2,1)} %shard_map.73), kind=kLoop, calls=%fused_computation | loop fusion | flops 524288 | bytes 2097152 | tf_op jit(solution)/shard_map/max | solution.py:310
